TPU v7x, 32 devices: a whole 2x2x4 slice. The times are simulated.
32 devices in a mesh: seq: 8 (over y, x, core), head: 4 (over z).
Axes of the slice: x: 2, y: 2, z: 4, core: 2. Of those that a mesh axis runs over, the one named last changes fastest.
Arguments:
- queries: bfloat16 [2048, 12288], P('seq', 'head'), may hold values from -256 to 256
- own_latent: bfloat16 [2048, 576], P('seq'), may hold values from -16 to 16
- cache: bfloat16 [256, 128, 576], P('seq', 'head'), may hold values from -6 to 6
- block_list: int32 [8, 32], replicated, may hold values from 0 to 255, as said below
- offsets: int32 [8, 32], P('seq'), may hold values from -4096 to 4096
- tile_mask: int32 [8, 2, 32], P('seq'), may hold values 0 or 1
- w_uk: bfloat16 [64, 128, 512], P('head'), may hold values from -0.5 to 0.5
- w_uv: bfloat16 [64, 512, 128], P('head'), may hold values from -0.25 to 0.25
- w_o: bfloat16 [8192, 7168], P('head'), may hold values from -0.0625 to 0.0625
Outputs:
- layer_out: bfloat16 [2048, 7168], P('seq', 'head')
Inputs may be any that keep to these rules, and one draw needn't show every extreme that they name: `block_list`: entry (r, j) names a pooled span whose owner is index entry // 32 of seq. In each row no owner is named more than 4 times, and at least one owner is named exactly 4 times.
All inputs are finite; a program needn't handle non-finite values. No bound on the sum of `tile_mask` on one device may be relied on, other than what follows from the above.
Results may differ from a plain program's by a relative error of at most 0.015.
Values may be sent and summed in bfloat16 or wider, within the bound.
A program may use at most 128 MiB of HBM per device.

v0:
```python
import jax
import jax.numpy as jnp
from jax import lax
from jax.sharding import PartitionSpec as P

MOST = 4


THETA = 50000.0


def rerotate(blocks, shift, latent_width):
    rotary_width = blocks.shape[-1] - latent_width
    halfway = rotary_width // 2
    inverse = THETA ** (-jnp.arange(halfway, dtype=jnp.float32) * 2.0 / rotary_width)
    angles = shift.astype(jnp.float32)[:, None] * inverse[None, :]
    cosine_table = jnp.cos(angles)[:, None, :]
    sine_table = jnp.sin(angles)[:, None, :]
    rotary = blocks[..., latent_width:].astype(jnp.float32)
    first_half = rotary[..., :halfway]
    second_half = rotary[..., halfway:]
    turned = jnp.concatenate(
        [
            first_half * cosine_table - second_half * sine_table,
            second_half * cosine_table + first_half * sine_table,
        ],
        axis=-1,
    )
    return jnp.concatenate([blocks[..., :latent_width], turned.astype(jnp.bfloat16)], axis=-1)


def allowed_keys(tiles, query_rows, block_rows):
    listed_mask = jnp.repeat(jnp.repeat(tiles > 0, block_rows, axis=0), block_rows, axis=1)
    causal = jnp.tril(jnp.ones((query_rows, query_rows), jnp.bool_))
    return jnp.concatenate([causal, listed_mask], axis=1)


def attend(grouped, context, allowed, key_maps, value_maps):
    nope_width = key_maps.shape[1]
    latent_width = key_maps.shape[2]
    factor = grouped.shape[-1] ** (-0.5)
    value_latent = context[:, :latent_width]

    def one_head(inputs):
        head_query, key_map, value_map = inputs
        query_latent = jnp.dot(
            head_query[:, :nope_width], key_map, preferred_element_type=jnp.float32
        ).astype(jnp.bfloat16)
        query_full = jnp.concatenate([query_latent, head_query[:, nope_width:]], axis=1)
        scores = (
            lax.dot_general(
                query_full, context, (((1,), (1,)), ((), ())), preferred_element_type=jnp.float32
            )
            * factor
        )
        scores = jnp.where(allowed, scores, -1e30)
        highest = jnp.max(scores, axis=1, keepdims=True)
        weights = jnp.exp(scores - highest)
        denominator = jnp.sum(weights, axis=1, keepdims=True)
        shares = (weights / denominator).astype(jnp.bfloat16)
        mixed_latent = jnp.dot(shares, value_latent, preferred_element_type=jnp.float32).astype(
            jnp.bfloat16
        )
        return jnp.dot(mixed_latent, value_map, preferred_element_type=jnp.float32).astype(
            jnp.bfloat16
        )

    per_head = lax.map(one_head, (jnp.transpose(grouped, (1, 0, 2)), key_maps, value_maps))
    return jnp.transpose(per_head, (1, 0, 2)).reshape(grouped.shape[0], -1)


def per_device(queries, own_latent, cache, block_list, offsets, tile_mask, w_uk, w_uv, w_o):
    seq_count = lax.axis_size("seq")
    seq_index = lax.axis_index("seq")
    spans_held = cache.shape[0]
    latent_full = cache.shape[2]
    listed_count = block_list.shape[1]
    owners = block_list // spans_held
    within = block_list % spans_held
    earlier = jnp.tril(jnp.ones((listed_count, listed_count), jnp.bool_), -1)
    same_owner = owners[:, :, None] == owners[:, None, :]
    ranking = jnp.sum(same_owner & earlier[None], axis=2)
    slot_ids = jnp.arange(MOST, dtype=jnp.int32)
    matches = (owners == seq_index)[:, :, None] & (ranking[:, :, None] == slot_ids[None, None, :])
    send_index = jnp.sum(jnp.where(matches, within[:, :, None], 0), axis=1)
    my_owners = lax.dynamic_index_in_dim(owners, seq_index, 0, keepdims=False)
    my_ranking = lax.dynamic_index_in_dim(ranking, seq_index, 0, keepdims=False)
    flat_slot = my_owners * MOST + my_ranking
    pooled = lax.all_gather(cache, "head", axis=1, tiled=True)
    arrived = lax.all_to_all(pooled[send_index], "seq", split_axis=0, concat_axis=0, tiled=True)
    blocks = arrived.reshape(seq_count * MOST, pooled.shape[1], latent_full)[flat_slot]
    latent_width = w_uk.shape[2]
    block_rows = blocks.shape[1]
    turned = rerotate(blocks, offsets[0], latent_width).reshape(
        listed_count * block_rows, latent_full
    )
    context = jnp.concatenate([own_latent, turned], axis=0)
    query_rows = own_latent.shape[0]
    allowed = allowed_keys(tile_mask[0], query_rows, block_rows)
    head_width = w_uk.shape[1] + latent_full - latent_width
    grouped = queries.reshape(query_rows, -1, head_width)
    head_out = attend(grouped, context, allowed, w_uk, w_uv)
    partial_value = jnp.dot(head_out, w_o, preferred_element_type=jnp.float32)
    result = lax.psum_scatter(
        partial_value.astype(jnp.bfloat16), "head", scatter_dimension=1, tiled=True
    )
    return result


def solution(mesh):
    placed = (
        P("seq", "head"),
        P("seq", None),
        P("seq", "head", None),
        P(),
        P("seq", None),
        P("seq", None, None),
        P("head", None, None),
        P("head", None, None),
        P("head", None),
    )
    return jax.shard_map(
        per_device, mesh=mesh, in_specs=placed, out_specs=P("seq", "head"), check_vma=False
    )
```

profile of v0, /device:TPU:2, one launch (start us, length us, event | category | flops | bytes accessed | tf_op | source)
XLA Modules:
  0.0 534.6 jit_solution(805157055343146215)
XLA Ops:
  9.4 98.9 %all-gather.2.cloned.1.call-done = bf16[32,128,576]{2,1,0:T(8,128)(2,1)} async-done(((bf16[32,32,576]{2,1,0:T(8,128)(2,1)}), bf16[32,128,576]{2,1,0:T(8,128)(2,1)}) %all-gather.2.cloned.1.call-update) | async-done | bytes 4718608 | tf_op jit(solution)/shard_map/all_gather | solution.py:89
  108.3 6.0 %gather_fusion = bf16[32,128,576]{2,1,0:T(8,128)(2,1)} fusion(bf16[32,128,576]{2,1,0:T(8,128)(2,1)} %all-gather.2.cloned.1.call-done, s32[1024]{0:T(1024)S(1)} %pad_clamp_fusion.1), kind=kCustom, calls=%fused_computation | custom fusion | bytes 9437312 | tf_op jit(solution)/shard_map/gather | solution.py:90
  114.2 7.6 %copy.26 = bf16[32,128,576]{1,2,0:T(8,128)(2,1)} copy(bf16[32,128,576]{2,1,0:T(8,128)(2,1)} %gather_fusion) | data formatting | bytes 9437184 | tf_op jit(solution)/shard_map/gather | solution.py:90
  121.8 5.2 all-to-all-start
  133.4 46.9 %all-to-all-done = bf16[8,4,128,576]{2,3,1,0:T(8,128)(2,1)} async-done(((bf16[8,4,128,576]{2,3,1,0:T(8,128)(2,1)}), bf16[8,4,128,576]{2,3,1,0:T(8,128)(2,1)}, u32[]{:S(2)}, u32[]{:S(2)}) %all-to-all-start) | async-done | bytes 4718624 | tf_op jit(solution)/shard_map/all_to_all | solution.py:90
  180.3 5.6 %gather_fusion.1 = bf16[32,128,576]{1,2,0:T(8,128)(2,1)} fusion(bf16[32,128,576]{1,2,0:T(8,128)(2,1)} %bitcast.8, s32[1024]{0:T(1024)S(1)} %pad_clamp_fusion), kind=kCustom, calls=%fused_computation.1 | custom fusion | bytes 9437312 | tf_op jit(solution)/shard_map/gather | solution.py:91
  189.3 2.3 pad_maximum_fusion.1
  191.6 7.6 %copy.27 = bf16[32,128,576]{2,1,0:T(8,128)(2,1)} copy(bf16[32,128,576]{1,2,0:T(8,128)(2,1)} %pad_maximum_fusion.1) | data formatting | bytes 9437184 | tf_op jit(solution)/shard_map/concatenate | solution.py:29
  199.2 5.6 %pad_maximum_fusion = bf16[4352,576]{1,0:T(8,128)(2,1)} fusion(bf16[256,576]{1,0:T(8,128)(2,1)S(1)} %copy.28, bf16[4096,576]{1,0:T(8,128)(2,1)} %bitcast.51), kind=kLoop, calls=%fused_computation.28 | loop fusion | flops 10027008 | bytes 10027008 | tf_op jit(solution)/shard_map/concatenate | solution.py:97
  204.8 2.5 fusion.18
  207.3 239.4 %while.10 = (s32[]{:T(128)}, bf16[16,256,128]{1,2,0:T(8,128)(2,1)}, bf16[16,256,192]{1,2,0:T(8,128)(2,1)S(1)}, bf16[16,128,512]{2,1,0:T(8,128)(2,1)}, bf16[4352,...) while((s32[]{:T(128)}, bf16[16,256,128]{1,2,0:T(8,128)(2,1)}, ...), condition=%wide.region_5.6_spmd, body=%wide.region_2.5_spmd.sunk | while | flops 2501213696 | bytes 43457148 | solution.py:68
  208.6 4.9 fusion.41
  216.4 5.1 fusion.43
  223.5 4.9 fusion.41
  228.5 2.1 copy-done
  231.3 5.1 fusion.43
  238.5 4.9 fusion.41
  243.4 2.1 copy-done
  246.3 5.1 fusion.43
  253.5 4.9 fusion.41
  258.4 2.1 copy-done
  261.3 5.1 fusion.43
  268.4 4.9 fusion.41
  276.2 5.1 fusion.43
  283.4 4.9 fusion.41
  291.2 5.1 fusion.43
  298.3 4.9 fusion.41
  306.2 5.1 fusion.43
  313.3 4.9 fusion.41
  321.1 5.1 fusion.43
  328.2 4.9 fusion.41
  336.1 5.1 fusion.43
  343.2 4.9 fusion.41
  351.0 5.1 fusion.43
  358.2 4.9 fusion.41
  366.0 5.1 fusion.43
  373.1 4.9 fusion.41
  380.9 5.1 fusion.43
  388.1 4.9 fusion.41
  395.9 5.1 fusion.43
  403.1 4.9 fusion.41
  410.9 5.1 fusion.43
  418.0 4.9 fusion.41
  425.8 5.1 fusion.43
  433.0 4.9 fusion.41
  440.8 5.1 fusion.43
  446.7 14.9 %convolution_convert_fusion.1 = bf16[256,7168]{1,0:T(8,128)(2,1)} fusion(bf16[256,2048]{0,1:T(8,128)(2,1)} %bitcast.59, bf16[2048,7168]{1,0:T(8,128)(2,1)} %param.19), kind=kOutput, calls=%fused_computation.26 | convolution fusion | flops 7518027776 | bytes 34078720 | tf_op jit(solution)/shard_map/dot_general | solution.py:103
  461.7 66.1 %reduce-scatter.2.cloned.1.call-done = bf16[256,1792]{1,0:T(8,128)(2,1)} async-done(((bf16[256,7168]{1,0:T(8,128)(2,1)}), bf16[256,1792]{1,0:T(8,128)(2,1)}) %reduce-scatter.2.cloned.1.call-update) | async-done | bytes 917520 | tf_op jit(solution)/shard_map/reduce_scatter | solution.py:104
  (181 shorter events, 83.6 us)
Async XLA Ops:
  6.5 101.7 %all-gather.2.cloned.1.call-start = ((), (), s32[]{:S(2)}) async-start(), calls=%async_computation.2 | async-start | bytes 6553600 | tf_op jit(solution)/shard_map/all_gather | solution.py:89
  121.8 5.2 copy-start.2
  121.8 5.4 %copy-start.3 = (s32[1,2,32]{2,1,0:T(2,128)S(1)}, s32[1,2,32]{2,1,0:T(2,128)}, u32[]{:S(2)}) copy-start(s32[1,2,32]{2,1,0:T(2,128)} %param.16) | copy-start | bytes 772
  121.8 58.5 %all-to-all-start = ((bf16[8,4,128,576]{2,3,1,0:T(8,128)(2,1)}), bf16[8,4,128,576]{2,3,1,0:T(8,128)(2,1)}, u32[]{:S(2)}, u32[]{:S(2)}) async-start(bf16[8,4,128,576]{2,3,1,0:T(8,128)(2,1)} %bitcast.53), calls=%async_computation | async-start | bytes 9437184 | tf_op jit(solution)/shard_map/all_to_all | solution.py:90
  127.0 4.9 copy-start.4
  127.0 400.8 %reduce-scatter.2.cloned.1.call-start = ((), (), s32[]{:S(2)}) async-start(), calls=%async_computation.3 | async-start | bytes 4587520 | tf_op jit(solution)/shard_map/reduce_scatter | solution.py:104
  187.1 2.2 slice-start
  199.2 5.6 %copy-start.1 = (bf16[32,128,576]{2,1,0:T(8,128)(2,1)S(1)}, bf16[32,128,576]{2,1,0:T(8,128)(2,1)}, u32[]{:S(2)}) copy-start(bf16[32,128,576]{2,1,0:T(8,128)(2,1)} %copy.27) | copy-start | bytes 14155780
  213.5 2.1 copy-start
  228.5 2.1 copy-start
  243.4 2.1 copy-start
  258.4 2.1 copy-start
  273.3 2.1 copy-start
  288.3 2.1 copy-start
  303.3 2.1 copy-start
  318.2 2.1 copy-start
  333.2 2.1 copy-start
  348.1 2.1 copy-start
  363.1 2.1 copy-start
  378.0 2.1 copy-start
  393.0 2.1 copy-start
  408.0 2.1 copy-start
  423.0 2.1 copy-start
  437.9 2.1 copy-start
Sparse Core Ops, SparseCore 0:
  8.9 99.2 all-gather.1
  461.8 65.9 reduce-scatter.1
where the time goes:
time: 537 us; the launch traced here: 535 us
  waiting for transfers between devices  213 us (40%)
  matrix products  194 us (36%)
  local copies, waits for them, and re-layouts  81.3 us (15%)
  other arithmetic  27.2 us (5%)
  between operations  13.6 us (3%)
    all_gather x1, waiting for transfers between devices, per_device(): pooled = lax.all_gather(cache, 'head', axis=1, tiled=True)  98.9 us
    dot_general x16, matrix products, one_head(): jnp.dot(mixed_latent, value_map, preferred_element_type=jnp.float32)  82.3 us
    dot_general x16, matrix products, one_head(): lax.dot_general(query_full, context, (((1,), (1,)), ((), ())), preferred_...  78.9 us
    reduce_scatter x1, waiting for transfers between devices, per_device(): lax.psum_scatter(partial_value.astype(jnp.bfloat16), 'head', scatter_dime...  66.1 us
    all_to_all x1, waiting for transfers between devices, per_device(): lax.all_to_all(pooled[send_index], 'seq', split_axis=0, concat_axis=0, ti...  46.9 us
    while x32, local copies, waits for them, and re-layouts  34.1 us
    dot_general x16, matrix products, one_head(): jnp.dot(head_query[:, :nope_width], key_map, preferred_element_type=jnp.f...  17.8 us
    dot_general x1, matrix products, per_device(): partial_value = jnp.dot(head_out, w_o, preferred_element_type=jnp.float32)  14.9 us
  transfers between devices with their start and end apart: 3, of which 3 were waited for; matrix products, arithmetic and copies ran while one was open for 2% of the time, Pallas kernels for 0%

commit v1 on v0

v1 whole, which is shorter than its diff:
```python
import functools
import math

import jax
import jax.numpy as jnp
from jax import lax
from jax.experimental import pallas as pl
from jax.experimental.pallas import tpu as pltpu
from jax.sharding import PartitionSpec as P

MOST = 4
THETA = 50000.0
MESH = pl.DeviceIdType.MESH
NEG = -1e30


def rotate(rotary, shift):
    width = rotary.shape[-1]
    halfway = width // 2
    inverse = THETA ** (-jnp.arange(halfway, dtype=jnp.float32) * 2.0 / width)
    angles = shift.astype(jnp.float32)[:, None] * inverse[None, :]
    cosine = jnp.cos(angles)[:, None, :]
    sine = jnp.sin(angles)[:, None, :]
    rotary = rotary.astype(jnp.float32)
    first = rotary[..., :halfway]
    second = rotary[..., halfway:]
    turned = jnp.concatenate(
        [first * cosine - second * sine, second * cosine + first * sine], axis=-1
    )
    return turned.astype(jnp.bfloat16)


def attention_kernel(
    n, group, scale,
    lat_in, rope_in, own_lat, own_rope, bias_in, qlat_in, qrest_in, wuv_in,
    out_ref,
    lat, rope, own_l, own_r, bias, qlat, qrest, wuv, acc, top, total,
    load_sem, recv_lat, recv_rope, send_lat, send_rope,
):
    seq = lax.axis_index("seq")
    me = lax.axis_index("head")
    heads, rows, width = qlat.shape
    keys = lat.shape[2]
    steps = heads // group

    mine = [
        pltpu.make_async_copy(lat_in, lat.at[me], load_sem.at[0]),
        pltpu.make_async_copy(rope_in, rope.at[me], load_sem.at[1]),
    ]
    rest = [
        pltpu.make_async_copy(src, dst, load_sem.at[2 + i])
        for i, (src, dst) in enumerate(
            [(own_lat, own_l), (own_rope, own_r), (bias_in, bias), (qlat_in, qlat),
             (qrest_in, qrest), (wuv_in, wuv)]
        )
    ]
    for copy in mine + rest:
        copy.start()

    barrier = pltpu.get_barrier_semaphore()

    @pl.when(me > 0)
    def _():
        pl.semaphore_signal(barrier, inc=1, device_id=(seq, me - 1), device_id_type=MESH)

    @pl.when(me < n - 1)
    def _():
        pl.semaphore_signal(barrier, inc=1, device_id=(seq, me + 1), device_id_type=MESH)

    peers = jnp.where(me > 0, 1, 0) + jnp.where(me < n - 1, 1, 0)
    pl.semaphore_wait(barrier, peers)

    for copy in mine:
        copy.wait()

    def latent_copy(origin, half, way):
        return pltpu.make_async_remote_copy(
            src_ref=lat.at[origin, half], dst_ref=lat.at[origin, half],
            send_sem=send_lat.at[way, origin, half], recv_sem=recv_lat.at[origin, half],
            device_id=(seq, me + (1 if way == 0 else -1)), device_id_type=MESH,
        )

    def rope_copy(origin, way):
        return pltpu.make_async_remote_copy(
            src_ref=rope.at[origin], dst_ref=rope.at[origin],
            send_sem=send_rope.at[way, origin], recv_sem=recv_rope.at[origin],
            device_id=(seq, me + (1 if way == 0 else -1)), device_id_type=MESH,
        )

    def can_send(way):
        return me < n - 1 if way == 0 else me > 0

    for way in range(2):
        @pl.when(can_send(way))
        def _():
            rope_copy(me, way).start()
            latent_copy(me, 0, way).start()
            latent_copy(me, 1, way).start()

    for copy in rest:
        copy.wait()

    def scores(g, variant, key):
        query = jnp.concatenate(
            [
                qlat[pl.ds(g * group, group)].reshape(group * rows, width),
                qrest[variant, pl.ds(g * group, group)].reshape(group * rows, -1),
            ],
            axis=1,
        )
        return lax.dot_general(
            query, key, (((1,), (1,)), ((), ())), preferred_element_type=jnp.float32
        )

    def own_step(g, carry):
        key = jnp.concatenate([own_l[...], own_r[...], jnp.zeros((rows, bias.shape[2]), own_r.dtype)], axis=1)
        s = scores(g, 0, key) * scale
        s = s.reshape(group, rows, rows)
        place = lax.broadcasted_iota(jnp.int32, (group, rows, rows), 1)
        column = lax.broadcasted_iota(jnp.int32, (group, rows, rows), 2)
        s = jnp.where(column <= place, s, NEG).reshape(group * rows, rows)
        high = jnp.max(s, axis=1, keepdims=True)
        p = jnp.exp2(s - high)
        span = pl.ds(g * group * rows, group * rows)
        top[span] = jnp.broadcast_to(high, (group * rows, top.shape[1]))
        total[span] = jnp.broadcast_to(
            jnp.sum(p, axis=1, keepdims=True), (group * rows, top.shape[1])
        )
        acc[span] = jnp.dot(
            p.astype(jnp.bfloat16), own_l[...], preferred_element_type=jnp.float32
        )
        return carry

    lax.fori_loop(0, steps, own_step, 0)

    def work(origin, half):
        def one(g, carry):
            value = lat[origin, half]
            key = jnp.concatenate([value, rope[origin], bias[half]], axis=1)
            s = scores(g, half, key)
            span = pl.ds(g * group * rows, group * rows)
            before = top[span][:, :1]
            high = jnp.maximum(before, jnp.max(s, axis=1, keepdims=True) * scale)
            p = jnp.exp2(s * scale - high)
            fade = jnp.exp2(before - high)
            top[span] = jnp.broadcast_to(high, (group * rows, top.shape[1]))
            total[span] = total[span] * fade + jnp.sum(p, axis=1, keepdims=True)
            acc[span] = acc[span] * fade + jnp.dot(
                p.astype(jnp.bfloat16), value, preferred_element_type=jnp.float32
            )
            return carry

        lax.fori_loop(0, steps, one, 0)

    def own_half(half, carry):
        work(me, half)
        return carry

    lax.fori_loop(0, 2, own_half, 0)

    def slot(k, carry):
        far = 1 + k // 2
        half = k % 2
        for way in range(2):
            origin = me - far if way == 0 else me + far
            here = origin >= 0 if way == 0 else origin < n

            @pl.when(here)
            def _():
                @pl.when(half == 0)
                def _():
                    rope_copy(origin, way).wait_recv()

                latent_copy(origin, half, way).wait_recv()

                @pl.when(can_send(way))
                def _():
                    @pl.when(half == 0)
                    def _():
                        rope_copy(origin, way).start()

                    latent_copy(origin, half, way).start()

        def side(way, carry):
            origin = jnp.where(way == 0, me - far, me + far)

            @pl.when(jnp.logical_and(origin >= 0, origin < n))
            def _():
                work(origin, half)

            return carry

        lax.fori_loop(0, 2, side, 0)
        return carry

    lax.fori_loop(0, 2 * (n - 1), slot, 0)

    def finish(h, carry):
        span = pl.ds(h * rows, rows)
        mixed = (acc[span] / total[span][:, :1]).astype(jnp.bfloat16)
        out_ref[h] = jnp.dot(
            mixed, wuv[h], preferred_element_type=jnp.float32
        ).astype(jnp.bfloat16)
        return carry

    lax.fori_loop(0, heads, finish, 0)

    for far in range(n):
        for way in range(2):
            origin = me - far if way == 0 else me + far
            here = origin >= 0 if way == 0 else origin < n

            @pl.when(jnp.logical_and(here, can_send(way)))
            def _():
                rope_copy(origin, way).wait_send()
                latent_copy(origin, 0, way).wait_send()
                latent_copy(origin, 1, way).wait_send()


def attention(n, scale, lat, rope, own_lat, own_rope, bias, qlat, qrest, wuv):
    heads, rows, width = qlat.shape
    keys = lat.shape[1]
    group = 2 if heads % 2 == 0 else 1
    bf = jnp.bfloat16
    every = heads * rows
    flops = 2 * every * (keys * 2 * n + rows) * (2 * width + rope.shape[1] // 2)
    return pl.pallas_call(
        functools.partial(attention_kernel, n, group, scale),
        out_shape=jax.ShapeDtypeStruct((heads, rows, wuv.shape[2]), bf),
        in_specs=[pl.BlockSpec(memory_space=pl.ANY)] * 8,
        out_specs=pl.BlockSpec(memory_space=pltpu.VMEM),
        scratch_shapes=[
            pltpu.VMEM((n,) + lat.shape, bf),
            pltpu.VMEM((n,) + rope.shape, bf),
            pltpu.VMEM(own_lat.shape, bf),
            pltpu.VMEM(own_rope.shape, bf),
            pltpu.VMEM(bias.shape, bf),
            pltpu.VMEM(qlat.shape, bf),
            pltpu.VMEM(qrest.shape, bf),
            pltpu.VMEM(wuv.shape, bf),
            pltpu.VMEM((every, width), jnp.float32),
            pltpu.VMEM((every, 128), jnp.float32),
            pltpu.VMEM((every, 128), jnp.float32),
            pltpu.SemaphoreType.DMA((8,)),
            pltpu.SemaphoreType.DMA((n, 2)),
            pltpu.SemaphoreType.DMA((n,)),
            pltpu.SemaphoreType.DMA((2, n, 2)),
            pltpu.SemaphoreType.DMA((2, n)),
        ],
        compiler_params=pltpu.CompilerParams(
            collective_id=0, has_side_effects=True, vmem_limit_bytes=56 * 1024 * 1024
        ),
        cost_estimate=pl.CostEstimate(
            flops=flops, bytes_accessed=16 * 1024 * 1024, transcendentals=every * keys * 2 * n
        ),
    )(lat, rope, own_lat, own_rope, bias, qlat, qrest, wuv)


def per_device(queries, own_latent, cache, block_list, offsets, tile_mask, w_uk, w_uv, w_o):
    seq_count = lax.axis_size("seq")
    n = lax.axis_size("head")
    seq_index = lax.axis_index("seq")
    spans_held, part_rows, full = cache.shape
    listed = block_list.shape[1]
    heads, nope, width = w_uk.shape
    rope_width = full - width
    rows = own_latent.shape[0]
    bf = jnp.bfloat16

    owners = block_list // spans_held
    within = block_list % spans_held
    earlier = jnp.tril(jnp.ones((listed, listed), jnp.bool_), -1)
    same_owner = owners[:, :, None] == owners[:, None, :]
    ranking = jnp.sum(same_owner & earlier[None], axis=2)
    slot_ids = jnp.arange(MOST, dtype=jnp.int32)
    matches = (owners == seq_index)[:, :, None] & (ranking[:, :, None] == slot_ids[None, None, :])
    send_index = jnp.sum(jnp.where(matches, within[:, :, None], 0), axis=1)
    my_owners = lax.dynamic_index_in_dim(owners, seq_index, 0, keepdims=False)
    my_ranking = lax.dynamic_index_in_dim(ranking, seq_index, 0, keepdims=False)
    flat_slot = my_owners * MOST + my_ranking
    arrived = lax.all_to_all(cache[send_index], "seq", split_axis=0, concat_axis=0, tiled=True)
    blocks = arrived.reshape(seq_count * MOST, part_rows, full)[flat_slot]

    keys = listed * part_rows // 2
    lat = blocks[..., :width].reshape(2, keys, width)
    turned = rotate(blocks[..., width:], offsets[0]).reshape(2, keys, rope_width)
    rope = jnp.concatenate([turned[0], turned[1]], axis=1)

    tiles = tile_mask[0]
    tile_count = tiles.shape[0]
    pad = 128
    penalty = jnp.where(tiles > 0, 0.0, NEG).astype(bf)
    bias = jnp.repeat(penalty.T, part_rows, axis=0).reshape(2, keys, tile_count)
    bias = jnp.pad(bias, ((0, 0), (0, 0), (0, pad - tile_count)))

    own_lat = own_latent[:, :width]
    own_rope = jnp.pad(own_latent[:, width:], ((0, 0), (0, rope_width)))

    grouped = jnp.transpose(queries.reshape(rows, heads, nope + rope_width), (1, 0, 2))
    qlat = jnp.einsum(
        "htn,hnl->htl", grouped[..., :nope], w_uk, preferred_element_type=jnp.float32
    ).astype(bf)
    qrope = grouped[..., nope:]
    nothing = jnp.zeros_like(qrope)
    tile_of = jnp.arange(rows) // (rows // tile_count)
    which = (tile_of[:, None] == jnp.arange(pad)[None, :]).astype(bf)
    which = jnp.broadcast_to(which[None], (heads, rows, pad))
    qrest = jnp.stack(
        [
            jnp.concatenate([qrope, nothing, which], axis=2),
            jnp.concatenate([nothing, qrope, which], axis=2),
        ]
    )
    scale = (nope + rope_width) ** -0.5 * math.log2(math.e)
    per_head = attention(n, scale, lat, rope, own_lat, own_rope, bias, qlat, qrest, w_uv)
    head_out = jnp.transpose(per_head, (1, 0, 2)).reshape(rows, -1)
    partial_value = jnp.dot(head_out, w_o, preferred_element_type=jnp.float32)
    return lax.psum_scatter(
        partial_value.astype(bf), "head", scatter_dimension=1, tiled=True
    )


def solution(mesh):
    placed = (
        P("seq", "head"),
        P("seq", None),
        P("seq", "head", None),
        P(),
        P("seq", None),
        P("seq", None, None),
        P("head", None, None),
        P("head", None, None),
        P("head", None),
    )
    return jax.shard_map(
        per_device, mesh=mesh, in_specs=placed, out_specs=P("seq", "head"), check_vma=False
    )
```

time: 537 us -> 258 us (0.48)
  matrix products: 194 us -> 18 us
  waiting for transfers between devices: 213 us -> 68.6 us
  Pallas kernels: 0 us -> 122 us
  local copies, waits for them, and re-layouts: 81.3 us -> 22.4 us
  other arithmetic: 27.2 us -> 7.76 us
    dot_general x48 -> x1, matrix products: 179 us -> 3.21 us  [per_device(): jnp.einsum('htn,hnl->htl', grouped[..., :nope], w_uk, preferred_element_t...]
    pallas_call x0 -> x1, Pallas kernels: none -> 122 us  [attention(): pl.pallas_call(functools.partial(attention_kernel, n, group, scale), out_...]
    all_gather x1 -> x0, waiting for transfers between devices: 98.9 us -> none  [per_device(): pooled = lax.all_gather(cache, 'head', axis=1, tiled=True)]
    all_to_all x1, waiting for transfers between devices: 46.9 us -> 0.01 us  [per_device(): lax.all_to_all(cache[send_index], 'seq', split_axis=0, concat_axis=0, til...]
    while x32 -> x0, local copies, waits for them, and re-layouts: 34.1 us -> none
    gather x3 -> x2, local copies, waits for them, and re-layouts: 19.2 us -> 3.96 us  [the longest x1 3.18 us: per_device(): cache[send_index]]
    reduce_sum x16 -> x0, other arithmetic: 11.9 us -> none  [one_head(): denominator = jnp.sum(weights, axis=1, keepdims=True)]
    dynamic_update_slice x32 -> x0, local copies, waits for them, and re-layouts: 11.8 us -> none  [attend(): lax.map(one_head, (jnp.transpose(grouped, (1, 0, 2)), key_maps, value_maps))]
  transfers between devices with their start and end apart: 3 -> 2, of which waited for: 3 -> 1; matrix products, arithmetic and copies ran while one was open for 2% -> 9% of each run, Pallas kernels for 0% -> 0%
where the time goes in v1:
time: 258 us; the launch traced here: 256 us
  Pallas kernels  122 us (47%)
  waiting for transfers between devices  68.6 us (27%)
  local copies, waits for them, and re-layouts  22.4 us (9%)
  matrix products  18 us (7%)
  between operations  13.6 us (5%)
  other arithmetic  7.76 us (3%)
  starting transfers between devices  4.26 us (2%)
    pallas_call x1, Pallas kernels, attention(): pl.pallas_call(functools.partial(attention_kernel, n, group, scale), out_...  122 us
    reduce_scatter x1, waiting for transfers between devices, per_device(): lax.psum_scatter(partial_value.astype(bf), 'head', scatter_dimension=1, t...  68.6 us
    dot_general x1, matrix products, per_device(): partial_value = jnp.dot(head_out, w_o, preferred_element_type=jnp.float32)  14.8 us
    unnamed x15, local copies, waits for them, and re-layouts  5.17 us
  transfers between devices with their start and end apart: 2, of which 1 were waited for; matrix products, arithmetic and copies ran while one was open for 9% of the time, Pallas kernels for 0%

profile of v1, /device:TPU:2, one launch (start us, length us, event | category | flops | bytes accessed | tf_op | source)
XLA Modules:
  0.0 256.1 jit_solution(6488466833032087345)
XLA Ops:
  6.5 0.0 copy-start
  6.5 0.8 add_select_fusion
  7.4 0.7 broadcast_compare_fusion
  8.1 0.1 iota_compare_fusion.2
  8.2 0.3 convert_reduce_fusion
  8.5 0.2 select_reduce_fusion
  8.6 0.1 copy.21
  8.7 0.1 reshape.184
  8.8 3.2 %gather_fusion = bf16[32,32,576]{2,1,0:T(8,128)(2,1)} fusion(bf16[32,32,576]{2,1,0:T(8,128)(2,1)} %param.11, s32[1024]{0:T(1024)S(1)} %pad_clamp_fusion.1), kind=kCustom, calls=%fused_computation | custom fusion | bytes 2359424 | tf_op jit(solution)/shard_map/gather | solution.py:281
  12.0 4.3 %all-to-all-start = ((bf16[8,4,32,576]{3,2,1,0:T(8,128)(2,1)}), bf16[8,4,32,576]{3,2,1,0:T(8,128)(2,1)S(1)}, u32[]{:S(2)}, u32[]{:S(2)}) async-start(bf16[8,4,32,576]{3,2,1,0:T(8,128)(2,1)} %bitcast.35), calls=%async_computation | async-start | bytes 2621440 | tf_op jit(solution)/shard_map/all_to_all | solution.py:281
  16.2 0.0 reduce-scatter.2.cloned.1.call-start
  16.3 1.7 slice.38
  17.9 2.6 %copy.25 = bf16[256,3072]{0,1:T(8,128)(2,1)} copy(bf16[256,3072]{1,0:T(8,128)(2,1)} %param.9) | data formatting | bytes 3145728 | tf_op args[0]
  20.6 3.7 %copy.26 = bf16[256,16,192]{2,0,1:T(8,128)(2,1)} copy(bf16[256,16,192]{0,2,1:T(8,128)(2,1)} %bitcast.33) | data formatting | bytes 3145728 | tf_op jit(solution)/shard_map/reshape | solution.py:299
  24.3 2.3 slice.53
  26.6 0.1 fusion.4
  26.7 0.0 copy-done.4
  26.7 0.1 copy.24
  26.8 1.8 copy.28.own_lat
  28.6 0.0 slice-done
  28.6 0.7 copy.29
  29.4 0.8 pad.9.bias_in
  30.1 1.5 pad.8.own_rope
  31.6 0.2 broadcast_in_dim.58
  31.8 0.2 broadcast_in_dim.35
  32.0 0.0 copy-done.3
  32.0 1.9 fusion
  33.9 0.0 copy-start.5
  33.9 0.0 copy-start.2
  34.0 2.3 pad_maximum_fusion.qrest_in
  36.3 0.0 copy-done.5
  36.3 0.1 multiply_cosine_fusion
  36.4 0.0 copy-done
  36.4 0.0 copy-done.2
  36.4 3.2 %convolution_convert_fusion.1.qlat_in = bf16[16,256,512]{2,1,0:T(8,128)(2,1)} fusion(bf16[16,128,512]{2,1,0:T(8,128)(2,1)S(1)} %copy-done, bf16[16,256,192]{2,1,0:T(8,128)(2,1)S(1)} %bitcast.32), kind=kOutput, calls=%fused_computation.6 | convolution fusion | flops 538968064 | bytes 7340032 | tf_op jit(solution)/shard_map/htn,hnl->htl/dot_general | solution.py:300
  39.7 0.0 all-to-all-done
  39.7 0.8 gather_fusion.1
  40.4 0.1 slice_convert_fusion
  40.5 1.2 slice.46
  41.7 0.2 subtract_convert_fusion
  41.9 0.1 fusion.3
  42.1 0.8 pad_maximum_fusion.4.rope_in
  42.8 121.5 %shard_map.91 = bf16[16,256,128]{2,1,0:T(8,128)(2,1)} custom-call(bf16[2,512,512]{2,1,0:T(8,128)(2,1)} %bitcast.38, bf16[512,128]{1,0:T(8,128)(2,1)} %pad_maximum_fusion.4.rope_in, bf16[256,512]{1,0:T(8,128)(2,1)} %copy.28.own_lat, bf16[256,128]{1,0:T(8,128)(2,1)} %pad.8.own_rope, bf16[2,512,128]{2,1,0:T(8,128)(2,1)} %pad.9.bias_in, ...), custom_call_target="tpu_custom_call" | custom-call | flops 38788923392 | bytes 16777216 | tf_op jit(solution)/shard_map/pallas_call | solution.py:227
  164.4 1.5 copy.27
  165.9 0.0 copy-start.1
  165.9 14.8 %convolution_convert_fusion = bf16[256,7168]{1,0:T(8,128)(2,1)} fusion(bf16[256,2048]{0,1:T(8,128)(2,1)S(1)} %bitcast.36, bf16[2048,7168]{1,0:T(8,128)(2,1)} %param.17), kind=kOutput, calls=%fused_computation.2 | convolution fusion | flops 7518027776 | bytes 34078720 | tf_op jit(solution)/shard_map/dot_general | solution.py:317
  180.7 0.0 reduce-scatter.2.cloned.1.call-update
  180.7 68.6 %reduce-scatter.2.cloned.1.call-done = bf16[256,1792]{1,0:T(8,128)(2,1)} async-done(((bf16[256,7168]{1,0:T(8,128)(2,1)}), bf16[256,1792]{1,0:T(8,128)(2,1)}) %reduce-scatter.2.cloned.1.call-update) | async-done | bytes 917520 | tf_op jit(solution)/shard_map/reduce_scatter | solution.py:318
  (14 shorter events, 0.1 us)
Async XLA Ops:
  6.5 29.9 %copy-start = (bf16[16,128,512]{2,1,0:T(8,128)(2,1)S(1)}, bf16[16,128,512]{2,1,0:T(8,128)(2,1)}, u32[]{:S(2)}) copy-start(bf16[16,128,512]{2,1,0:T(8,128)(2,1)} %param.15) | copy-start | bytes 6291460
  12.0 27.7 %all-to-all-start = ((bf16[8,4,32,576]{3,2,1,0:T(8,128)(2,1)}), bf16[8,4,32,576]{3,2,1,0:T(8,128)(2,1)S(1)}, u32[]{:S(2)}, u32[]{:S(2)}) async-start(bf16[8,4,32,576]{3,2,1,0:T(8,128)(2,1)} %bitcast.35), calls=%async_computation | async-start | bytes 2621440 | tf_op jit(solution)/shard_map/all_to_all | solution.py:281
  16.2 233.0 %reduce-scatter.2.cloned.1.call-start = ((), (), s32[]{:S(2)}) async-start(), calls=%async_computation.2 | async-start | bytes 4587520 | tf_op jit(solution)/shard_map/reduce_scatter | solution.py:318
  20.6 6.1 %copy-start.4 = (s32[1,2,32]{2,1,0:T(2,128)S(1)}, s32[1,2,32]{2,1,0:T(2,128)}, u32[]{:S(2)}) copy-start(s32[1,2,32]{2,1,0:T(2,128)} %param.14) | copy-start | bytes 772
  24.2 4.4 %slice-start = ((bf16[256,576]{0,1:T(8,128)(2,1)}), bf16[256,64]{0,1:T(8,128)(2,1)S(1)}, s32[]{:S(2)}) async-start(bf16[256,576]{0,1:T(8,128)(2,1)} %param.10), calls=%async_computation.3 | async-start | bytes 65536 | tf_op jit(solution)/shard_map/slice | solution.py:297
  29.3 2.7 %copy-start.3 = (bf16[16,256,64]{2,1,0:T(8,128)(2,1)S(1)}, bf16[16,256,64]{2,1,0:T(8,128)(2,1)}, u32[]{:S(2)}) copy-start(bf16[16,256,64]{2,1,0:T(8,128)(2,1)} %slice.53) | copy-start | bytes 1572868
  33.9 2.3 copy-start.5
  33.9 2.5 copy-start.2
  165.9 83.4 %copy-start.1 = (bf16[16,128,512]{2,1,0:T(8,128)(2,1)S(1)}, bf16[16,128,512]{2,1,0:T(8,128)(2,1)}, u32[]{:S(2)}) copy-start(bf16[16,128,512]{2,1,0:T(8,128)(2,1)} %param.15) | copy-start | bytes 6291460
Sparse Core Ops, SparseCore 0:
  180.8 68.4 reduce-scatter.1

commit v2 on v1

--- a/solution.py
+++ b/solution.py
@@ -42,6 +42,7 @@
     heads, rows, width = qlat.shape
     keys = lat.shape[2]
     steps = heads // group
+    batch = 4 if steps % 4 == 0 else 1
 
     mine = [
         pltpu.make_async_copy(lat_in, lat.at[me], load_sem.at[0]),
@@ -134,10 +135,10 @@
     lax.fori_loop(0, steps, own_step, 0)
 
     def work(origin, half):
-        def one(g, carry):
-            value = lat[origin, half]
-            key = jnp.concatenate([value, rope[origin], bias[half]], axis=1)
-            s = scores(g, half, key)
+        value = lat[origin, half]
+        key = jnp.concatenate([value, rope[origin], bias[half]], axis=1)
+
+        def soft(g, s):
             span = pl.ds(g * group * rows, group * rows)
             before = top[span][:, :1]
             high = jnp.maximum(before, jnp.max(s, axis=1, keepdims=True) * scale)
@@ -148,9 +149,17 @@
             acc[span] = acc[span] * fade + jnp.dot(
                 p.astype(jnp.bfloat16), value, preferred_element_type=jnp.float32
             )
+
+        def some(i, carry):
+            ahead = scores(i * batch, half, key)
+            for j in range(batch):
+                s = ahead
+                if j + 1 < batch:
+                    ahead = scores(i * batch + j + 1, half, key)
+                soft(i * batch + j, s)
             return carry
 
-        lax.fori_loop(0, steps, one, 0)
+        lax.fori_loop(0, steps // batch, some, 0)
 
     def own_half(half, carry):
         work(me, half)
@@ -198,7 +207,9 @@
     def finish(h, carry):
         span = pl.ds(h * rows, rows)
         mixed = (acc[span] / total[span][:, :1]).astype(jnp.bfloat16)
-        out_ref[h] = jnp.dot(
+        value_width = wuv.shape[2]
+        columns = pl.ds(pl.multiple_of(h * value_width, value_width), value_width)
+        out_ref[:, columns] = jnp.dot(
             mixed, wuv[h], preferred_element_type=jnp.float32
         ).astype(jnp.bfloat16)
         return carry
@@ -226,7 +237,7 @@
     flops = 2 * every * (keys * 2 * n + rows) * (2 * width + rope.shape[1] // 2)
     return pl.pallas_call(
         functools.partial(attention_kernel, n, group, scale),
-        out_shape=jax.ShapeDtypeStruct((heads, rows, wuv.shape[2]), bf),
+        out_shape=jax.ShapeDtypeStruct((rows, heads * wuv.shape[2]), bf),
         in_specs=[pl.BlockSpec(memory_space=pl.ANY)] * 8,
         out_specs=pl.BlockSpec(memory_space=pltpu.VMEM),
         scratch_shapes=[
@@ -256,6 +267,162 @@
     )(lat, rope, own_lat, own_rope, bias, qlat, qrest, wuv)
 
 
+def project_kernel(
+    n, head_out, w_o, out_ref, weight, part, inbox, weight_sem, send_sem, recv_sem
+):
+    seq = lax.axis_index("seq")
+    me = lax.axis_index("head")
+    rows, wide = out_ref.shape
+    tile = 256 if wide % 256 == 0 else 128
+
+    def block_of(p):
+        return jnp.where(2 * me < n, n - 1 - p, p)
+
+    def fetch(p):
+        columns = pl.ds(pl.multiple_of(block_of(p) * wide, 128), wide)
+        return pltpu.make_async_copy(
+            w_o.at[:, columns], weight.at[p % 2], weight_sem.at[p % 2]
+        )
+
+    fetch(0).start()
+    barrier = pltpu.get_barrier_semaphore()
+
+    @pl.when(me > 0)
+    def _():
+        pl.semaphore_signal(barrier, inc=1, device_id=(seq, me - 1), device_id_type=MESH)
+
+    @pl.when(me < n - 1)
+    def _():
+        pl.semaphore_signal(barrier, inc=1, device_id=(seq, me + 1), device_id_type=MESH)
+
+    peers = jnp.where(me > 0, 1, 0) + jnp.where(me < n - 1, 1, 0)
+    pl.semaphore_wait(barrier, peers)
+
+    def first(block, way):
+        return pltpu.make_async_remote_copy(
+            src_ref=part.at[block], dst_ref=inbox.at[way, block],
+            send_sem=send_sem.at[way, block], recv_sem=recv_sem.at[way, block],
+            device_id=(seq, me + (1 if way == 0 else -1)), device_id_type=MESH,
+        )
+
+    def onward(block, way):
+        return pltpu.make_async_remote_copy(
+            src_ref=inbox.at[way, block], dst_ref=inbox.at[way, block],
+            send_sem=send_sem.at[way, block], recv_sem=recv_sem.at[way, block],
+            device_id=(seq, me + (1 if way == 0 else -1)), device_id_type=MESH,
+        )
+
+    def compute(p, carry):
+        block = block_of(p)
+
+        @pl.when(p + 1 < n)
+        def _():
+            fetch(p + 1).start()
+
+        fetch(p).wait()
+
+        def columns_step(t, carry):
+            columns = pl.ds(pl.multiple_of(t * tile, tile), tile)
+            part[block, :, columns] = jnp.dot(
+                head_out[...], weight[p % 2, :, columns], preferred_element_type=jnp.float32
+            ).astype(jnp.bfloat16)
+            return carry
+
+        lax.fori_loop(0, wide // tile, columns_step, 0)
+
+        @pl.when(jnp.logical_and(me == 0, block > 0))
+        def _():
+            first(block, 0).start()
+
+        @pl.when(jnp.logical_and(me == n - 1, block < n - 1))
+        def _():
+            first(block, 1).start()
+
+        return carry
+
+    lax.fori_loop(0, n, compute, 0)
+
+    def hop(k, carry):
+        for way in range(2):
+            block = n - 1 + me - k if way == 0 else k - (n - 1 - me)
+            if way == 0:
+                here = jnp.logical_and(me > 0, jnp.logical_and(block > me, block < n))
+            else:
+                here = jnp.logical_and(me < n - 1, jnp.logical_and(block >= 0, block < me))
+
+            @pl.when(here)
+            def _():
+                onward(block, way).wait_recv()
+                inbox[way, block] = (
+                    inbox[way, block].astype(jnp.float32) + part[block].astype(jnp.float32)
+                ).astype(jnp.bfloat16)
+                onward(block, way).start()
+
+        return carry
+
+    lax.fori_loop(1, n - 1, hop, 0)
+
+    @pl.when(me == 0)
+    def _():
+        first(me, 1).wait_recv()
+        out_ref[...] = (
+            part[me].astype(jnp.float32) + inbox[1, me].astype(jnp.float32)
+        ).astype(jnp.bfloat16)
+
+    @pl.when(me == n - 1)
+    def _():
+        first(me, 0).wait_recv()
+        out_ref[...] = (
+            part[me].astype(jnp.float32) + inbox[0, me].astype(jnp.float32)
+        ).astype(jnp.bfloat16)
+
+    @pl.when(jnp.logical_and(me > 0, me < n - 1))
+    def _():
+        first(me, 0).wait_recv()
+        first(me, 1).wait_recv()
+        out_ref[...] = (
+            part[me].astype(jnp.float32)
+            + inbox[0, me].astype(jnp.float32)
+            + inbox[1, me].astype(jnp.float32)
+        ).astype(jnp.bfloat16)
+
+    for block in range(n):
+        @pl.when(block > me)
+        def _():
+            first(block, 0).wait_send()
+
+        @pl.when(block < me)
+        def _():
+            first(block, 1).wait_send()
+
+
+def project(n, head_out, w_o):
+    rows, depth = head_out.shape
+    wide = w_o.shape[1] // n
+    bf = jnp.bfloat16
+    return pl.pallas_call(
+        functools.partial(project_kernel, n),
+        out_shape=jax.ShapeDtypeStruct((rows, wide), bf),
+        in_specs=[pl.BlockSpec(memory_space=pltpu.VMEM), pl.BlockSpec(memory_space=pl.ANY)],
+        out_specs=pl.BlockSpec(memory_space=pltpu.VMEM),
+        scratch_shapes=[
+            pltpu.VMEM((2, depth, wide), bf),
+            pltpu.VMEM((n, rows, wide), bf),
+            pltpu.VMEM((2, n, rows, wide), bf),
+            pltpu.SemaphoreType.DMA((2,)),
+            pltpu.SemaphoreType.DMA((2, n)),
+            pltpu.SemaphoreType.DMA((2, n)),
+        ],
+        compiler_params=pltpu.CompilerParams(
+            collective_id=1, has_side_effects=True, vmem_limit_bytes=48 * 1024 * 1024
+        ),
+        cost_estimate=pl.CostEstimate(
+            flops=2 * rows * depth * wide * n, bytes_accessed=2 * depth * wide * n,
+            transcendentals=0,
+        ),
+    )(head_out, w_o)
+
+
 def per_device(queries, own_latent, cache, block_list, offsets, tile_mask, w_uk, w_uv, w_o):
     seq_count = lax.axis_size("seq")
     n = lax.axis_size("head")
@@ -312,12 +479,8 @@
         ]
     )
     scale = (nope + rope_width) ** -0.5 * math.log2(math.e)
-    per_head = attention(n, scale, lat, rope, own_lat, own_rope, bias, qlat, qrest, w_uv)
-    head_out = jnp.transpose(per_head, (1, 0, 2)).reshape(rows, -1)
-    partial_value = jnp.dot(head_out, w_o, preferred_element_type=jnp.float32)
-    return lax.psum_scatter(
-        partial_value.astype(bf), "head", scatter_dimension=1, tiled=True
-    )
+    head_out = attention(n, scale, lat, rope, own_lat, own_rope, bias, qlat, qrest, w_uv)
+    return project(n, head_out, w_o)
 
 
 def solution(mesh):

time: 258 us -> 213 us (0.83)
  waiting for transfers between devices: 68.6 us -> 0.01 us
  Pallas kernels: 122 us -> 169 us
  matrix products: 18 us -> 3.21 us
  between operations: 13.6 us -> 0.18 us
  local copies, waits for them, and re-layouts: 22.4 us -> 25.3 us
    reduce_scatter x1 -> x0, waiting for transfers between devices: 68.6 us -> none  [per_device(): lax.psum_scatter(partial_value.astype(bf), 'head', scatter_dimension=1, t...]
    pallas_call x0 -> x1, Pallas kernels: none -> 68.5 us  [project(): pl.pallas_call(functools.partial(project_kernel, n), out_shape=jax.ShapeD...]
    pallas_call x1, Pallas kernels: 122 us -> 100 us  [attention(): pl.pallas_call(functools.partial(attention_kernel, n, group, scale), out_...]
    dot_general x1 -> x0, matrix products: 14.8 us -> none  [per_device(): partial_value = jnp.dot(head_out, w_o, preferred_element_type=jnp.float32)]
    unnamed x15 -> x16, local copies, waits for them, and re-layouts: 5.17 us -> 7.3 us
  transfers between devices with their start and end apart: 2 -> 1, of which waited for: 1 -> 0; matrix products, arithmetic and copies ran while one was open for 9% -> 11% of each run, Pallas kernels for 0% -> 0%
where the time goes in v2:
time: 213 us; the launch traced here: 211 us
  Pallas kernels  169 us (79%)
  local copies, waits for them, and re-layouts  25.3 us (12%)
  other arithmetic  8.7 us (4%)
  starting transfers between devices  4.25 us (2%)
  matrix products  3.21 us (2%)
    pallas_call x1, Pallas kernels, attention(): pl.pallas_call(functools.partial(attention_kernel, n, group, scale), out_...  100 us
    pallas_call x1, Pallas kernels, project(): pl.pallas_call(functools.partial(project_kernel, n), out_shape=jax.ShapeD...  68.5 us
    unnamed x16, local copies, waits for them, and re-layouts  7.3 us
  transfers between devices with their start and end apart: 1, of which 0 were waited for; matrix products, arithmetic and copies ran while one was open for 11% of the time, Pallas kernels for 0%

profile of v2, /device:TPU:2, one launch (start us, length us, event | category | flops | bytes accessed | tf_op | source)
XLA Modules:
  0.0 210.6 jit_solution(12354708492914906501)
XLA Ops:
  0.0 0.0 copy-start
  0.0 0.8 add_select_fusion
  0.9 0.7 broadcast_compare_fusion
  1.5 0.1 iota_compare_fusion.2
  1.6 0.3 convert_reduce_fusion
  1.9 0.2 select_reduce_fusion
  2.1 0.1 copy.20
  2.2 0.1 reshape.180
  2.3 3.2 %gather_fusion = bf16[32,32,576]{2,1,0:T(8,128)(2,1)} fusion(bf16[32,32,576]{2,1,0:T(8,128)(2,1)} %param.11, s32[1024]{0:T(1024)S(1)} %pad_clamp_fusion.1), kind=kCustom, calls=%fused_computation | custom fusion | bytes 2359424 | tf_op jit(solution)/shard_map/gather | solution.py:448
  5.4 4.3 %all-to-all-start = ((bf16[8,4,32,576]{3,2,1,0:T(8,128)(2,1)}), bf16[8,4,32,576]{3,2,1,0:T(8,128)(2,1)S(1)}, u32[]{:S(2)}, u32[]{:S(2)}) async-start(bf16[8,4,32,576]{3,2,1,0:T(8,128)(2,1)} %bitcast.31), calls=%async_computation | async-start | bytes 2621440 | tf_op jit(solution)/shard_map/all_to_all | solution.py:448
  9.7 1.7 slice.38
  11.4 2.6 %copy.24 = bf16[256,3072]{0,1:T(8,128)(2,1)} copy(bf16[256,3072]{1,0:T(8,128)(2,1)} %param.9) | data formatting | bytes 3145728 | tf_op args[0]
  14.0 0.0 copy-start.4
  14.0 3.7 %copy.25 = bf16[256,16,192]{2,0,1:T(8,128)(2,1)} copy(bf16[256,16,192]{0,2,1:T(8,128)(2,1)} %bitcast.29) | data formatting | bytes 3145728 | tf_op jit(solution)/shard_map/reshape | solution.py:466
  17.7 0.0 slice-start
  17.7 2.3 %slice.53 = bf16[16,256,64]{2,1,0:T(8,128)(2,1)} slice(bf16[16,256,192]{2,1,0:T(8,128)(2,1)} %bitcast.27), slice={[0:16], [0:256], [128:192]} | slice | bytes 1048576 | tf_op jit(solution)/shard_map/slice | solution.py:470
  20.0 0.1 fusion.4
  20.1 0.0 copy-done.4
  20.2 0.1 copy.23
  20.3 1.8 copy.26.own_lat
  22.1 0.0 slice-done
  22.1 0.7 copy.27
  22.8 0.8 pad.9.bias_in
  23.6 1.5 pad.8.own_rope
  25.1 0.2 broadcast_in_dim.58
  25.3 0.2 broadcast_in_dim.35
  25.5 0.0 copy-done.3
  25.5 1.9 fusion
  27.4 0.0 copy-start.5
  27.4 0.0 copy-start.2
  27.4 2.3 %pad_maximum_fusion.qrest_in = bf16[2,16,256,256]{3,2,1,0:T(8,128)(2,1)} fusion(bf16[1,16,256,256]{3,2,1,0:T(8,128)(2,1)S(1)} %get-tuple-element.8, bf16[1,16,256,256]{3,2,1,0:T(8,128)(2,1)S(1)} %get-tuple-element.7), kind=kLoop, calls=%fused_computation.2 | loop fusion | flops 2097152 | bytes 8388608 | tf_op jit(solution)/shard_map/stack | solution.py:475
  29.7 0.0 copy-done.5
  29.7 0.1 multiply_cosine_fusion
  29.9 0.0 copy-done
  29.9 0.0 copy-done.2
  29.9 3.2 %convolution_convert_fusion.qlat_in = bf16[16,256,512]{2,1,0:T(8,128)(2,1)} fusion(bf16[16,128,512]{2,1,0:T(8,128)(2,1)S(1)} %copy-done, bf16[16,256,192]{2,1,0:T(8,128)(2,1)S(1)} %bitcast.28), kind=kOutput, calls=%fused_computation.5 | convolution fusion | flops 538968064 | bytes 7340032 | tf_op jit(solution)/shard_map/htn,hnl->htl/dot_general | solution.py:467
  33.1 0.0 all-to-all-done
  33.1 1.9 gather_fusion.1
  35.0 1.0 slice_convert_fusion
  36.0 2.3 %slice.46 = bf16[32,32,512]{2,1,0:T(8,128)(2,1)} slice(bf16[32,32,576]{2,1,0:T(8,128)(2,1)} %gather_fusion.1), slice={[0:32], [0:32], [0:512]} | slice | bytes 2097152 | tf_op jit(solution)/shard_map/slice | solution.py:452
  38.3 0.2 subtract_convert_fusion
  38.5 0.1 fusion.3
  38.7 0.8 pad_maximum_fusion.4.rope_in
  39.5 100.5 %shard_map.91.head_out = bf16[256,2048]{1,0:T(8,128)(2,1)} custom-call(bf16[2,512,512]{2,1,0:T(8,128)(2,1)} %bitcast.33, bf16[512,128]{1,0:T(8,128)(2,1)} %pad_maximum_fusion.4.rope_in, bf16[256,512]{1,0:T(8,128)(2,1)} %copy.26.own_lat, bf16[256,128]{1,0:T(8,128)(2,1)} %pad.8.own_rope, bf16[2,512,128]{2,1,0:T(8,128)(2,1)} %pad.9.bias_in, ...), custom_call_target="tpu_custom_call" | custom-call | flops 38788923392 | bytes 16777216 | tf_op jit(solution)/shard_map/pallas_call | solution.py:238
  139.9 0.0 copy-start.1
  139.9 1.2 copy-done.1
  141.2 68.5 %shard_map.92 = bf16[256,1792]{1,0:T(8,128)(2,1)S(1)} custom-call(bf16[256,2048]{1,0:T(8,128)(2,1)S(1)} %copy-done.1, bf16[2048,7168]{1,0:T(8,128)(2,1)} %w_o.1), custom_call_target="tpu_custom_call" | custom-call | flops 7516192768 | bytes 29360128 | tf_op jit(solution)/shard_map/pallas_call | solution.py:403
  209.7 0.9 copy.29
  (11 shorter events, 0.1 us)
Async XLA Ops:
  0.0 29.9 %copy-start = (bf16[16,128,512]{2,1,0:T(8,128)(2,1)S(1)}, bf16[16,128,512]{2,1,0:T(8,128)(2,1)}, u32[]{:S(2)}) copy-start(bf16[16,128,512]{2,1,0:T(8,128)(2,1)} %param.15) | copy-start | bytes 6291460
  5.4 27.7 %all-to-all-start = ((bf16[8,4,32,576]{3,2,1,0:T(8,128)(2,1)}), bf16[8,4,32,576]{3,2,1,0:T(8,128)(2,1)S(1)}, u32[]{:S(2)}, u32[]{:S(2)}) async-start(bf16[8,4,32,576]{3,2,1,0:T(8,128)(2,1)} %bitcast.31), calls=%async_computation | async-start | bytes 2621440 | tf_op jit(solution)/shard_map/all_to_all | solution.py:448
  14.0 6.1 %copy-start.4 = (s32[1,2,32]{2,1,0:T(2,128)S(1)}, s32[1,2,32]{2,1,0:T(2,128)}, u32[]{:S(2)}) copy-start(s32[1,2,32]{2,1,0:T(2,128)} %param.14) | copy-start | bytes 772
  17.7 4.4 %slice-start = ((bf16[256,576]{0,1:T(8,128)(2,1)}), bf16[256,64]{0,1:T(8,128)(2,1)S(1)}, s32[]{:S(2)}) async-start(bf16[256,576]{0,1:T(8,128)(2,1)} %param.10), calls=%async_computation.1 | async-start | bytes 65536 | tf_op jit(solution)/shard_map/slice | solution.py:464
  22.8 2.7 %copy-start.3 = (bf16[16,256,64]{2,1,0:T(8,128)(2,1)S(1)}, bf16[16,256,64]{2,1,0:T(8,128)(2,1)}, u32[]{:S(2)}) copy-start(bf16[16,256,64]{2,1,0:T(8,128)(2,1)} %slice.53) | copy-start | bytes 1572868
  27.4 2.3 %copy-start.5 = (s32[1,32]{1,0:T(1,128)S(1)}, s32[1,32]{1,0:T(1,128)}, u32[]{:S(2)}) copy-start(s32[1,32]{1,0:T(1,128)} %param.13) | copy-start | bytes 388
  27.4 2.5 %copy-start.2 = (bf16[256,16,192]{2,0,1:T(8,128)(2,1)S(1)}, bf16[256,16,192]{2,0,1:T(8,128)(2,1)}, u32[]{:S(2)}) copy-start(bf16[256,16,192]{2,0,1:T(8,128)(2,1)} %copy.25) | copy-start | bytes 4718596
  139.9 1.2 copy-start.1

commit v3 on v2

--- a/solution.py
+++ b/solution.py
@@ -31,10 +31,10 @@
 
 
 def attention_kernel(
-    n, group, scale,
-    lat_in, rope_in, own_lat, own_rope, bias_in, qlat_in, qrest_in, wuv_in,
+    n, group, tile_rows, scale,
+    lat_in, rope_in, own_lat, own_rope, bias_in, queries_in, wuk_in, wuv_in,
     out_ref,
-    lat, rope, own_l, own_r, bias, qlat, qrest, wuv, acc, top, total,
+    lat, rope, own_l, own_r, bias, queries, wuk, qlat, qrest, wuv, acc, top, total,
     load_sem, recv_lat, recv_rope, send_lat, send_rope,
 ):
     seq = lax.axis_index("seq")
@@ -51,8 +51,8 @@
     rest = [
         pltpu.make_async_copy(src, dst, load_sem.at[2 + i])
         for i, (src, dst) in enumerate(
-            [(own_lat, own_l), (own_rope, own_r), (bias_in, bias), (qlat_in, qlat),
-             (qrest_in, qrest), (wuv_in, wuv)]
+            [(own_lat, own_l), (own_rope, own_r), (bias_in, bias), (queries_in, queries),
+             (wuk_in, wuk), (wuv_in, wuv)]
         )
     ]
     for copy in mine + rest:
@@ -100,6 +100,35 @@
 
     for copy in rest:
         copy.wait()
+
+    nope = wuk.shape[1]
+    rope_width = nope // 2
+    pair_width = 3 * nope
+    tiles = bias_in.shape[2]
+    lane = lax.broadcasted_iota(jnp.int32, (rows, nope), 1)
+    mark_row = lax.broadcasted_iota(jnp.int32, (rows, tiles), 0)
+    mark_lane = lax.broadcasted_iota(jnp.int32, (rows, tiles), 1)
+    mark = jnp.where(mark_row // tile_rows == mark_lane, 1.0, 0.0).astype(jnp.bfloat16)
+
+    def prepare(i, carry):
+        even, odd = 2 * i, 2 * i + 1
+        x = queries[:, pl.ds(pl.multiple_of(i * pair_width, 128), pair_width)]
+        tail = x[:, nope:].astype(jnp.float32)
+        moved = pltpu.roll(tail, 2 * nope - rope_width, 1)
+        for h, plain, low, high in (
+            (even, x[:, :nope], tail[:, :nope], moved[:, nope:]),
+            (odd, moved[:, :nope].astype(jnp.bfloat16), moved[:, nope:], tail[:, nope:]),
+        ):
+            qlat[h] = jnp.dot(
+                plain, wuk[h], preferred_element_type=jnp.float32
+            ).astype(jnp.bfloat16)
+            first = jnp.where(lane < rope_width, low, 0.0).astype(jnp.bfloat16)
+            second = jnp.where(lane >= rope_width, high, 0.0).astype(jnp.bfloat16)
+            qrest[0, h] = jnp.concatenate([first, mark], axis=1)
+            qrest[1, h] = jnp.concatenate([second, mark], axis=1)
+        return carry
+
+    lax.fori_loop(0, heads // 2, prepare, 0)
 
     def scores(g, variant, key):
         query = jnp.concatenate(
@@ -228,15 +257,16 @@
                 latent_copy(origin, 1, way).wait_send()
 
 
-def attention(n, scale, lat, rope, own_lat, own_rope, bias, qlat, qrest, wuv):
-    heads, rows, width = qlat.shape
+def attention(n, tile_rows, scale, lat, rope, own_lat, own_rope, bias, queries, wuk, wuv):
+    heads, _, width = wuk.shape
+    rows = queries.shape[0]
     keys = lat.shape[1]
     group = 2 if heads % 2 == 0 else 1
     bf = jnp.bfloat16
     every = heads * rows
     flops = 2 * every * (keys * 2 * n + rows) * (2 * width + rope.shape[1] // 2)
     return pl.pallas_call(
-        functools.partial(attention_kernel, n, group, scale),
+        functools.partial(attention_kernel, n, group, tile_rows, scale),
         out_shape=jax.ShapeDtypeStruct((rows, heads * wuv.shape[2]), bf),
         in_specs=[pl.BlockSpec(memory_space=pl.ANY)] * 8,
         out_specs=pl.BlockSpec(memory_space=pltpu.VMEM),
@@ -246,8 +276,10 @@
             pltpu.VMEM(own_lat.shape, bf),
             pltpu.VMEM(own_rope.shape, bf),
             pltpu.VMEM(bias.shape, bf),
-            pltpu.VMEM(qlat.shape, bf),
-            pltpu.VMEM(qrest.shape, bf),
+            pltpu.VMEM(queries.shape, bf),
+            pltpu.VMEM(wuk.shape, bf),
+            pltpu.VMEM((heads, rows, width), bf),
+            pltpu.VMEM((2, heads, rows, rope.shape[1] + bias.shape[2]), bf),
             pltpu.VMEM(wuv.shape, bf),
             pltpu.VMEM((every, width), jnp.float32),
             pltpu.VMEM((every, 128), jnp.float32),
@@ -264,7 +296,7 @@
         cost_estimate=pl.CostEstimate(
             flops=flops, bytes_accessed=16 * 1024 * 1024, transcendentals=every * keys * 2 * n
         ),
-    )(lat, rope, own_lat, own_rope, bias, qlat, qrest, wuv)
+    )(lat, rope, own_lat, own_rope, bias, queries, wuk, wuv)
 
 
 def project_kernel(
@@ -463,23 +495,10 @@
     own_lat = own_latent[:, :width]
     own_rope = jnp.pad(own_latent[:, width:], ((0, 0), (0, rope_width)))
 
-    grouped = jnp.transpose(queries.reshape(rows, heads, nope + rope_width), (1, 0, 2))
-    qlat = jnp.einsum(
-        "htn,hnl->htl", grouped[..., :nope], w_uk, preferred_element_type=jnp.float32
-    ).astype(bf)
-    qrope = grouped[..., nope:]
-    nothing = jnp.zeros_like(qrope)
-    tile_of = jnp.arange(rows) // (rows // tile_count)
-    which = (tile_of[:, None] == jnp.arange(pad)[None, :]).astype(bf)
-    which = jnp.broadcast_to(which[None], (heads, rows, pad))
-    qrest = jnp.stack(
-        [
-            jnp.concatenate([qrope, nothing, which], axis=2),
-            jnp.concatenate([nothing, qrope, which], axis=2),
-        ]
+    scale = (nope + rope_width) ** -0.5 * math.log2(math.e)
+    head_out = attention(
+        n, rows // tile_count, scale, lat, rope, own_lat, own_rope, bias, queries, w_uk, w_uv
     )
-    scale = (nope + rope_width) ** -0.5 * math.log2(math.e)
-    head_out = attention(n, scale, lat, rope, own_lat, own_rope, bias, qlat, qrest, w_uv)
     return project(n, head_out, w_o)
 
 

time: 213 us -> 203 us (0.953); the launches traced: 211 us -> 203 us
  local copies, waits for them, and re-layouts: 25.3 us -> 10.7 us
  waiting for transfers between devices: 0.01 us -> 14 us
  other arithmetic: 8.7 us -> 4.35 us
  matrix products: 3.21 us -> 0 us
    all_to_all x1, waiting for transfers between devices: 0.01 us -> 14 us  [per_device(): lax.all_to_all(cache[send_index], 'seq', split_axis=0, concat_axis=0, til...]
    another operation x3 -> x1, other arithmetic: 4.43 us -> 0.22 us  [the longest x2 4.21 us: per_device(): jnp.stack([jnp.concatenate([qrope, nothing, which], axis=2), jnp.concaten...]
    unnamed x16 -> x11, local copies, waits for them, and re-layouts: 7.3 us -> 3.11 us
    reshape x1 -> x0, local copies, waits for them, and re-layouts: 3.69 us -> none  [per_device(): queries.reshape(rows, heads, nope + rope_width)]
    dot_general x1 -> x0, matrix products: 3.21 us -> none  [per_device(): jnp.einsum('htn,hnl->htl', grouped[..., :nope], w_uk, preferred_element_t...]
    slice x1 -> x0, local copies, waits for them, and re-layouts: 2.32 us -> none  [per_device(): qrope = grouped[..., nope:]]
  transfers between devices with their start and end apart: 1 -> 1, of which waited for: 0 -> 1; matrix products, arithmetic and copies ran while one was open for 11% -> 1% of each run, Pallas kernels for 0% -> 0%
where the time goes in v3:
time: 203 us
  Pallas kernels  170 us (84%)
  waiting for transfers between devices  14 us (7%)
  local copies, waits for them, and re-layouts  10.7 us (5%)
  starting transfers between devices  4.39 us (2%)
  other arithmetic  4.35 us (2%)
    pallas_call x1, Pallas kernels, attention(): pl.pallas_call(functools.partial(attention_kernel, n, group, tile_rows, s...  101 us
    pallas_call x1, Pallas kernels, project(): pl.pallas_call(functools.partial(project_kernel, n), out_shape=jax.ShapeD...  68.3 us
    all_to_all x1, waiting for transfers between devices, per_device(): lax.all_to_all(cache[send_index], 'seq', split_axis=0, concat_axis=0, til...  14 us
    all_to_all x1, starting transfers between devices, per_device(): lax.all_to_all(cache[send_index], 'seq', split_axis=0, concat_axis=0, til...  4.39 us
  transfers between devices with their start and end apart: 1, of which 1 were waited for; matrix products, arithmetic and copies ran while one was open for 1% of the time, Pallas kernels for 0%

profile of v3, /device:TPU:2, one launch (start us, length us, event | category | flops | bytes accessed | tf_op | source)
XLA Modules:
  0.0 203.2 jit_solution(3447989756052115140)
XLA Ops:
  0.0 0.0 copy-start
  0.0 0.8 add_select_fusion
  0.8 0.7 broadcast_compare_fusion
  1.5 0.1 iota_compare_fusion.1
  1.6 0.3 convert_reduce_fusion
  1.9 0.2 select_reduce_fusion
  2.0 0.1 copy.18
  2.1 0.1 reshape.143
  2.2 0.0 copy-done
  2.2 1.8 gather_fusion
  4.0 0.0 copy-start.2
  4.0 0.0 slice-start
  4.0 0.0 slice-start.1
  4.0 4.4 %all-to-all-start = ((bf16[8,4,32,576]{3,2,1,0:T(8,128)(2,1)}), bf16[8,4,32,576]{3,2,1,0:T(8,128)(2,1)S(1)}, u32[]{:S(2)}, u32[]{:S(2)}) async-start(bf16[8,4,32,576]{3,2,1,0:T(8,128)(2,1)} %bitcast.21), calls=%async_computation | async-start | bytes 2621440 | tf_op jit(solution)/shard_map/all_to_all | solution.py:480
  8.4 0.0 copy-start.3
  8.4 0.0 copy-done.2
  8.4 0.1 copy.21
  8.5 0.0 slice-done
  8.5 0.8 copy.22.own_lat
  9.4 0.0 slice-done.1
  9.4 0.1 copy.23
  9.5 0.8 pad.9.bias_in
  10.3 0.6 pad.8.own_rope
  11.0 0.0 copy-done.3
  11.0 0.1 multiply_cosine_fusion
  11.1 14.0 %all-to-all-done = bf16[8,4,32,576]{3,2,1,0:T(8,128)(2,1)S(1)} async-done(((bf16[8,4,32,576]{3,2,1,0:T(8,128)(2,1)}), bf16[8,4,32,576]{3,2,1,0:T(8,128)(2,1)S(1)}, u32[]{:S(2)}, u32[]{:S(2)}) %all-to-all-start) | async-done | bytes 1179680 | tf_op jit(solution)/shard_map/all_to_all | solution.py:480
  25.1 1.8 gather_fusion.1
  26.9 1.0 slice_convert_fusion
  27.9 2.3 %slice.38 = bf16[32,32,512]{2,1,0:T(8,128)(2,1)} slice(bf16[32,32,576]{2,1,0:T(8,128)(2,1)} %gather_fusion.1), slice={[0:32], [0:32], [0:512]} | slice | bytes 2097152 | tf_op jit(solution)/shard_map/slice | solution.py:484
  30.2 0.2 subtract_convert_fusion
  30.4 0.1 fusion
  30.6 0.8 pad_maximum_fusion.1.rope_in
  31.3 101.3 %shard_map.91.head_out = bf16[256,2048]{1,0:T(8,128)(2,1)} custom-call(bf16[2,512,512]{2,1,0:T(8,128)(2,1)} %bitcast.23, bf16[512,128]{1,0:T(8,128)(2,1)} %pad_maximum_fusion.1.rope_in, bf16[256,512]{1,0:T(8,128)(2,1)} %copy.22.own_lat, bf16[256,128]{1,0:T(8,128)(2,1)} %pad.8.own_rope, bf16[2,512,128]{2,1,0:T(8,128)(2,1)} %pad.9.bias_in, ...), custom_call_target="tpu_custom_call" | custom-call | flops 38788923392 | bytes 16777216 | tf_op jit(solution)/shard_map/pallas_call | solution.py:268
  132.7 0.0 copy-start.1
  132.7 1.2 copy-done.1
  133.9 68.3 %shard_map.92 = bf16[256,1792]{1,0:T(8,128)(2,1)S(1)} custom-call(bf16[256,2048]{1,0:T(8,128)(2,1)S(1)} %copy-done.1, bf16[2048,7168]{1,0:T(8,128)(2,1)} %w_o.1), custom_call_target="tpu_custom_call" | custom-call | flops 7516192768 | bytes 29360128 | tf_op jit(solution)/shard_map/pallas_call | solution.py:435
  202.2 0.9 copy.25
  (9 shorter events, 0.1 us)
Async XLA Ops:
  0.0 2.2 %copy-start = (bf16[32,32,576]{2,1,0:T(8,128)(2,1)S(1)}, bf16[32,32,576]{2,1,0:T(8,128)(2,1)}, u32[]{:S(2)}) copy-start(bf16[32,32,576]{2,1,0:T(8,128)(2,1)} %param.11) | copy-start | bytes 3538948
  4.0 4.4 %copy-start.2 = (s32[1,2,32]{2,1,0:T(2,128)S(1)}, s32[1,2,32]{2,1,0:T(2,128)}, u32[]{:S(2)}) copy-start(s32[1,2,32]{2,1,0:T(2,128)} %param.14) | copy-start | bytes 772
  4.0 4.5 %slice-start = ((bf16[256,576]{0,1:T(8,128)(2,1)}), bf16[256,512]{0,1:T(8,128)(2,1)S(1)}, s32[]{:S(2)}) async-start(bf16[256,576]{0,1:T(8,128)(2,1)} %param.10), calls=%async_computation.1 | async-start | bytes 524288 | tf_op jit(solution)/shard_map/slice | solution.py:495
  4.0 5.4 %slice-start.1 = ((bf16[256,576]{0,1:T(8,128)(2,1)}), bf16[256,64]{0,1:T(8,128)(2,1)S(1)}, s32[]{:S(2)}) async-start(bf16[256,576]{0,1:T(8,128)(2,1)} %param.10), calls=%async_computation.2 | async-start | bytes 65536 | tf_op jit(solution)/shard_map/slice | solution.py:496
  4.0 21.1 %all-to-all-start = ((bf16[8,4,32,576]{3,2,1,0:T(8,128)(2,1)}), bf16[8,4,32,576]{3,2,1,0:T(8,128)(2,1)S(1)}, u32[]{:S(2)}, u32[]{:S(2)}) async-start(bf16[8,4,32,576]{3,2,1,0:T(8,128)(2,1)} %bitcast.21), calls=%async_computation | async-start | bytes 2621440 | tf_op jit(solution)/shard_map/all_to_all | solution.py:480
  8.4 2.6 %copy-start.3 = (s32[1,32]{1,0:T(1,128)S(1)}, s32[1,32]{1,0:T(1,128)}, u32[]{:S(2)}) copy-start(s32[1,32]{1,0:T(1,128)} %param.13) | copy-start | bytes 388
  132.7 1.2 copy-start.1
